TPU v7x, 32 devices: a whole 2x2x4 slice. The times are simulated.
32 devices in a mesh: grp: 2 (over x), dom: 16 (over z, y, core).
Axes of the slice: x: 2, y: 2, z: 4, core: 2. Of those that a mesh axis runs over, the one named last changes fastest.
Arguments:
- conn: int32 [2, 16, 27, 512], P('grp', 'dom'), may hold values from 0 to 5119, as said below
- live: int32 [2, 16, 512], P('grp', 'dom'), may hold values from 0 to 1, as said below
- stiffness: float32 [2, 16, 512], P('grp', 'dom'), may hold values from 1 to 10
- owner: int32 [2, 16, 5120], P('grp', 'dom'), may hold values from 0 to 1, as said below
- free: int32 [2, 16, 5120], P('grp', 'dom'), may hold values from 0 to 1, as said below
- x_faces: int32 [2, 16, 2, 384], P('grp', 'dom'), may hold values from 0 to 5119, as said below
- peer_table: int32 [2, 256, 640], P('grp', 'dom'), may hold values from 0 to 5119, as said below
- disp: float32 [2, 16, 3, 5120], P('grp', 'dom'), may hold values from -0.024 to 0.024
- load: float32 [2, 16, 3, 5120], P('grp', 'dom'), may hold values from -15 to 15
Outputs:
- update: float32 [2, 16, 3, 5120], P('grp', 'dom')
- residual: float32 [2, 16, 3, 5120], P('grp', 'dom')
Inputs may be any that keep to these rules, and one draw needn't show every extreme that they name: `conn`: for a live slot the column lists the local ids of the element's 27 nodes, node a at offset (a // 9, a // 3 % 3, a % 3) half-sides from the element's lowest corner along (x, y, z); elements fill each device's box of 8 x 16 x 4 cubes, and the boxes tile the specimen, grp index along x, dom index = 8 * (box along y) + (box along z). A padded slot lists 5120 - 1, an id that is no node. Live slots come before padded ones on every device; some device has all 512 slots live. `owner`: exactly one copy of every mesh node has 1; ids that are no node have 0. `free`: 1 exactly on nodes that touch a live element and do not lie on the face x = 0 of the specimen, equal on all copies of a node; 0 on ids that are no node. `x_faces`: row 1 of a device and row 0 of the device with the next grp index and the same dom index list the same nodes in the same order; padding is 5119. `peer_table`: row q of device p and row p of device q (same grp index) list the nodes the two boxes share, in the same order, padded with 5119; a row is all padding unless the dom indices differ by 1, 7, 8 or 9.
All inputs are finite; a program needn't handle non-finite values.
Results may differ from a plain program's by a relative error of at most 0.00011.
Values sent between devices are 32-bit elements; how exact they have to be, the bound alone decides.
A program may use at most 128 MiB of HBM per device.

v0:
```python
import math

import jax
import jax.numpy as jnp
import numpy as np
from jax import lax
from jax.sharding import PartitionSpec as P

ITERS = 2


def from_behind(value, axis, steps):
    count = lax.axis_size(axis)
    leading, last = (max(0, -steps), min(count, count - steps))
    return lax.ppermute(value, axis, [(source, source + steps) for source in range(leading, last)])


def lagrange_values(place):
    return np.array([place * (place - 1.0) / 2.0, 1.0 - place * place, place * (place + 1.0) / 2.0])


def lagrange_slopes(place):
    return np.array([place - 0.5, -2.0 * place, place + 0.5])


def basis_tables():
    points = [-math.sqrt(0.6), 0.0, math.sqrt(0.6)]
    weights = [5.0 / 9.0, 8.0 / 9.0, 5.0 / 9.0]
    values = np.stack([lagrange_values(place) for place in points])
    slopes = np.stack([lagrange_slopes(place) for place in points])
    gradient_table = np.zeros((3, 27, 27))
    quad_weight = np.zeros(27)
    for point_index in range(27):
        first, second, third = (point_index // 9, point_index // 3 % 3, point_index % 3)
        quad_weight[point_index] = weights[first] * weights[second] * weights[third]
        for node_index in range(27):
            along_x, along_y, along_z = (node_index // 9, node_index // 3 % 3, node_index % 3)
            gradient_table[0, point_index, node_index] = (
                slopes[first, along_x] * values[second, along_y] * values[third, along_z]
            )
            gradient_table[1, point_index, node_index] = (
                values[first, along_x] * slopes[second, along_y] * values[third, along_z]
            )
            gradient_table[2, point_index, node_index] = (
                values[first, along_x] * values[second, along_y] * slopes[third, along_z]
            )
    return (
        jnp.asarray(gradient_table.reshape(81, 27), jnp.float32),
        jnp.asarray(quad_weight.reshape(27, 1), jnp.float32),
    )


def element_terms(
    gradient_table, quad_weight, nodal_state, nodal_probe, shear_modulus, lame_first, tangent
):
    block_size = nodal_state.shape[2]
    identity = jnp.eye(3, dtype=jnp.float32)[:, :, None, None]
    deform = identity + jnp.einsum(
        "ma,cab->cmb", gradient_table, nodal_state, precision=lax.Precision.HIGHEST
    ).reshape(3, 3, 27, block_size)
    volume = jnp.sum(deform[0] * jnp.cross(deform[1], deform[2], axis=0), axis=0)
    inverse = (
        jnp.stack(
            [
                jnp.cross(deform[1], deform[2], axis=0),
                jnp.cross(deform[2], deform[0], axis=0),
                jnp.cross(deform[0], deform[1], axis=0),
            ],
            axis=1,
        )
        / volume
    )
    inverse_t = jnp.swapaxes(inverse, 0, 1)
    log_volume = jnp.log(volume)
    if tangent:
        change = jnp.einsum(
            "ma,cab->cmb", gradient_table, nodal_probe, precision=lax.Precision.HIGHEST
        ).reshape(3, 3, 27, block_size)
        product = jnp.sum(inverse[:, :, None] * change[None], axis=1)
        twisted = jnp.sum(product[:, :, None] * inverse[None], axis=1)
        trace_term = product[0, 0] + product[1, 1] + product[2, 2]
        stress = (
            shear_modulus * change
            + (shear_modulus - lame_first * log_volume) * jnp.swapaxes(twisted, 0, 1)
            + lame_first * trace_term * inverse_t
        )
    else:
        stress = shear_modulus * (deform - inverse_t) + lame_first * log_volume * inverse_t
    weighted = (stress * quad_weight).reshape(3, 81, block_size)
    return jnp.einsum("ma,cmb->cab", gradient_table, weighted, precision=lax.Precision.HIGHEST)


def local_forces(
    gradient_table,
    quad_weight,
    connect,
    shear_modulus,
    lame_first,
    state_field,
    probe_field,
    tangent,
    block_count,
):

    def accumulate(block_index, summed_force):
        contribution = element_terms(
            gradient_table,
            quad_weight,
            state_field[:, connect],
            probe_field[:, connect],
            shear_modulus,
            lame_first,
            tangent,
        )
        return summed_force.at[:, connect].add(contribution)

    return lax.fori_loop(0, block_count, accumulate, jnp.zeros(state_field.shape, jnp.float32))


def assemble(field, faces, peer_rows):
    lower_ids = faces[0]
    upper_ids = faces[1]
    from_below = from_behind(field[:, upper_ids], "grp", 1)
    from_above = from_behind(field[:, lower_ids], "grp", -1)
    summed = field.at[:, lower_ids].add(from_below).at[:, upper_ids].add(from_above)
    arrived = lax.all_to_all(summed[:, peer_rows], "dom", split_axis=1, concat_axis=1, tiled=True)
    total_field = summed.at[:, peer_rows].add(arrived)
    return total_field


def single_product(owner_weight, first_field, second_field):
    return lax.psum(jnp.sum(owner_weight * first_field * second_field), ("grp", "dom"))


def per_device(conn, live, stiffness, owner, free, x_faces, peer_table, disp, load):
    gradient_table, quad_weight = basis_tables()
    connect = conn[0, 0]
    live_flags = live[0, 0]
    live_weight = live_flags.astype(jnp.float32)
    shear_modulus = live_weight * stiffness[0, 0] / 2.6
    lame_first = live_weight * stiffness[0, 0] * 0.3 / 0.52
    owner_weight = owner[0, 0].astype(jnp.float32)
    free_weight = free[0, 0].astype(jnp.float32)
    faces = x_faces[0, 0]
    peer_rows = peer_table[0]
    slot_count = connect.shape[1]
    block_size = min(slot_count, 512)
    block_count = slot_count // block_size
    state_field = assemble(owner_weight * disp[0, 0], faces, peer_rows)
    internal_force = local_forces(
        gradient_table,
        quad_weight,
        connect,
        shear_modulus,
        lame_first,
        state_field,
        state_field,
        False,
        block_count,
    )
    right_side = free_weight * assemble(
        owner_weight * load[0, 0] - internal_force, faces, peer_rows
    )
    solution = jnp.zeros_like(right_side)
    residual = right_side
    direction = right_side
    norm_now = single_product(owner_weight, residual, residual)
    for iteration in range(ITERS):
        applied = local_forces(
            gradient_table,
            quad_weight,
            connect,
            shear_modulus,
            lame_first,
            state_field,
            direction,
            True,
            block_count,
        )
        image_field = free_weight * assemble(applied, faces, peer_rows)
        step_length = norm_now / single_product(owner_weight, direction, image_field)
        solution = solution + step_length * direction
        residual = residual - step_length * image_field
        if iteration + 1 < ITERS:
            norm_next = single_product(owner_weight, residual, residual)
            direction = residual + norm_next / norm_now * direction
            norm_now = norm_next
    return (solution[None, None], residual[None, None])


def solution(mesh):
    in_specs = (
        P("grp", "dom", None, None),
        P("grp", "dom", None),
        P("grp", "dom", None),
        P("grp", "dom", None),
        P("grp", "dom", None),
        P("grp", "dom", None, None),
        P("grp", "dom", None),
        P("grp", "dom", None, None),
        P("grp", "dom", None, None),
    )
    out_specs = (P("grp", "dom", None, None), P("grp", "dom", None, None))
    return jax.shard_map(
        per_device, mesh=mesh, in_specs=in_specs, out_specs=out_specs, check_vma=False
    )
```

profile of v0, /device:TPU:0, one launch (start us, length us, event | category | flops | bytes accessed | tf_op | source)
XLA Modules:
  0.0 1168.8 jit_solution(15500046756285150080)
XLA Ops:
  28.4 34.3 %gather_fusion.2 = f32[10240,3]{1,0:T(8,128)} fusion(f32[3,5120]{0,1:T(8,128)S(1)} %scatter_custom_fusion.1, s32[10240]{0:T(1024)S(1)} %broadcast_clamp_fusion), kind=kCustom, calls=%fused_computation.2 | custom fusion | bytes 286720 | tf_op jit(solution)/shard_map/gather | solution.py:126
  75.0 6.1 all-to-all-done
  84.2 71.5 %scatter_fusion = f32[3,5120]{0,1:T(8,128)S(1)} fusion(f32[3,5120]{0,1:T(8,128)S(1)} %scatter_custom_fusion.1, s32[10240]{0:T(1024)S(1)} %reshape.588, f32[10240,3]{1,0:T(8,128)} %copy.102), kind=kCustom, calls=%fused_computation.17 | custom fusion | flops 30720 | bytes 409600 | tf_op jit(solution)/shard_map/scatter-add | solution.py:127
  155.7 26.1 %gather_fusion.3 = f32[13824,3]{1,0:T(8,128)} fusion(f32[3,5120]{0,1:T(8,128)S(1)} %scatter_fusion, s32[14336]{0:T(1024)S(1)} %pad_clamp_fusion), kind=kCustom, calls=%fused_computation.3 | custom fusion | bytes 387072 | tf_op jit(solution)/shard_map/while/body/eval_jaxpr/gather | solution.py:109
  193.1 87.5 %scatter_custom_fusion.3 = f32[3,5120]{0,1:T(8,128)} fusion(s32[13824]{0:T(1024)} %copy-done.4, f32[13824,3]{1,0:T(8,128)} %bitcast.199, f32[]{:T(128)} %constant.22.clone.1), kind=kCustom, calls=%fused_computation.52 | custom fusion | flops 41472 | bytes 61952 | tf_op jit(solution)/shard_map/while/body/eval_jaxpr/scatter-add | solution.py:115
  305.0 34.3 %gather_fusion.6 = f32[10240,3]{1,0:T(8,128)} fusion(f32[3,5120]{0,1:T(8,128)S(1)} %scatter_custom_fusion.5, s32[10240]{0:T(1024)S(1)} %broadcast_clamp_fusion), kind=kCustom, calls=%fused_computation.6 | custom fusion | bytes 286720 | tf_op jit(solution)/shard_map/gather | solution.py:126
  348.1 7.7 all-to-all-done.1
  359.8 71.3 %scatter_fusion.1 = f32[3,5120]{0,1:T(8,128)S(1)} fusion(f32[3,5120]{0,1:T(8,128)S(1)} %scatter_custom_fusion.5, s32[10240]{0:T(1024)S(1)} %reshape.588, f32[10240,3]{1,0:T(8,128)} %copy.111), kind=kCustom, calls=%fused_computation.21 | custom fusion | flops 30720 | bytes 409600 | tf_op jit(solution)/shard_map/scatter-add | solution.py:127
  434.4 27.8 %gather_fusion.7 = f32[13824,3]{1,0:T(8,128)} fusion(f32[3,5120]{0,1:T(8,128)} %broadcast_multiply_fusion, s32[14336]{0:T(1024)S(1)} %pad_clamp_fusion), kind=kCustom, calls=%fused_computation.7 | custom fusion | bytes 387072 | tf_op jit(solution)/shard_map/while/body/eval_jaxpr/gather | solution.py:110
  484.1 87.5 %scatter_custom_fusion.7 = f32[3,5120]{0,1:T(8,128)} fusion(s32[13824]{0:T(1024)} %copy-done.4, f32[13824,3]{1,0:T(8,128)} %bitcast.200, f32[]{:T(128)} %constant.22.clone.1), kind=kCustom, calls=%fused_computation.50 | custom fusion | flops 41472 | bytes 61952 | tf_op jit(solution)/shard_map/while/body/eval_jaxpr/scatter-add | solution.py:115
  586.7 6.2 scatter_custom_fusion.8
  592.9 6.2 scatter_custom_fusion.9
  599.1 36.0 %gather_fusion.10 = f32[10240,3]{1,0:T(8,128)} fusion(f32[3,5120]{0,1:T(8,128)} %scatter_custom_fusion.9, s32[10240]{0:T(1024)S(1)} %broadcast_clamp_fusion), kind=kCustom, calls=%fused_computation.10 | custom fusion | bytes 286720 | tf_op jit(solution)/shard_map/gather | solution.py:126
  639.0 12.8 %all_to_all.20 = f32[3,16,640]{2,0,1:T(4,128)} all-to-all(f32[3,16,640]{2,0,1:T(4,128)} %bitcast.218), channel_id=1, replica_groups=mesh['grp'=2,'dom'=16] {'dom'}, dimensions={1} | all-to-all | bytes 245760 | tf_op jit(solution)/shard_map/all_to_all | solution.py:126
  655.8 72.9 %scatter_fusion.2 = f32[3,5120]{0,1:T(8,128)} fusion(f32[3,5120]{0,1:T(8,128)} %scatter_custom_fusion.9, s32[10240]{0:T(1024)S(1)} %reshape.588, f32[10240,3]{1,0:T(8,128)} %copy.119), kind=kCustom, calls=%fused_computation.25 | custom fusion | flops 30720 | bytes 409600 | tf_op jit(solution)/shard_map/scatter-add | solution.py:127
  733.6 38.2 %all-reduce = (f32[]{:T(128)}, f32[]{:T(128)}) all-reduce(f32[]{:T(128)} %get-tuple-element.76, f32[]{:T(128)} %get-tuple-element.75), channel_id=1, replica_groups=mesh['grp'=2,'dom'=16] {'grp','dom'}, use_global_device_ids=true, to_apply=%region_9.0 | all-reduce | flops 2 | bytes 16 | tf_op jit(solution)/shard_map/psum | solution.py:132
  778.0 42.6 %psum.30 = f32[]{:T(128)} all-reduce(f32[]{:T(128)} %fusion.2), channel_id=1, replica_groups=mesh['grp'=2,'dom'=16] {'grp','dom'}, use_global_device_ids=true, to_apply=%region_19.0 | all-reduce | flops 1 | bytes 8 | tf_op jit(solution)/shard_map/psum | solution.py:132
  826.5 27.8 %gather_fusion.11 = f32[13824,3]{1,0:T(8,128)} fusion(f32[3,5120]{0,1:T(8,128)} %multiply_add_fusion, s32[14336]{0:T(1024)S(1)} %pad_clamp_fusion), kind=kCustom, calls=%fused_computation.11 | custom fusion | bytes 387072 | tf_op jit(solution)/shard_map/while/body/eval_jaxpr/gather | solution.py:110
  872.7 87.5 %scatter_custom_fusion.11 = f32[3,5120]{0,1:T(8,128)} fusion(s32[13824]{0:T(1024)} %copy-done.4, f32[13824,3]{1,0:T(8,128)} %bitcast.198, f32[]{:T(128)} %constant.22.clone.1), kind=kCustom, calls=%fused_computation.48 | custom fusion | flops 41472 | bytes 61952 | tf_op jit(solution)/shard_map/while/body/eval_jaxpr/scatter-add | solution.py:115
  986.7 36.0 %gather_fusion.14 = f32[10240,3]{1,0:T(8,128)} fusion(f32[3,5120]{0,1:T(8,128)} %scatter_custom_fusion.13, s32[10240]{0:T(1024)S(1)} %broadcast_clamp_fusion), kind=kCustom, calls=%fused_computation.14 | custom fusion | bytes 286720 | tf_op jit(solution)/shard_map/gather | solution.py:126
  1026.0 11.1 all_to_all.21
  1040.2 73.0 %scatter_fusion.3 = f32[3,5120]{0,1:T(8,128)} fusion(f32[3,5120]{0,1:T(8,128)} %scatter_custom_fusion.13, s32[10240]{0:T(1024)S(1)} %reshape.588, f32[10240,3]{1,0:T(8,128)} %copy.125), kind=kCustom, calls=%fused_computation.29 | custom fusion | flops 30720 | bytes 409600 | tf_op jit(solution)/shard_map/scatter-add | solution.py:127
  1118.3 38.1 %psum.31 = f32[]{:T(128)} all-reduce(f32[]{:T(128)} %multiply_reduce_fusion), channel_id=1, replica_groups=mesh['grp'=2,'dom'=16] {'grp','dom'}, use_global_device_ids=true, to_apply=%region_27.29 | all-reduce | flops 1 | bytes 8 | tf_op jit(solution)/shard_map/psum | solution.py:132
  1157.7 6.0 subtract_bitcast_fusion
  (132 shorter events, 215.1 us)
Async XLA Ops:
  1.4 294.4 %copy-start.9 = (s32[384]{0:T(512)}, s32[384]{0:T(512)S(1)}, u32[]{:S(2)}) copy-start(s32[384]{0:T(512)S(1)} %get-tuple-element.87) | copy-start | bytes 4612
  1.4 299.4 %copy-start.8 = (s32[384]{0:T(512)}, s32[384]{0:T(512)S(1)}, u32[]{:S(2)}) copy-start(s32[384]{0:T(512)S(1)} %get-tuple-element.86) | copy-start | bytes 4612
  5.3 12.5 %copy-start.7 = (s32[1,16,640]{2,1,0:T(8,128)S(1)}, s32[1,16,640]{2,1,0:T(8,128)}, u32[]{:S(2)}) copy-start(s32[1,16,640]{2,1,0:T(8,128)} %param.19) | copy-start | bytes 122884
  5.3 12.5 %copy-start.13 = (f32[1,1,512]{2,1,0:T(1,128)S(1)}, f32[1,1,512]{2,1,0:T(1,128)}, u32[]{:S(2)}) copy-start(f32[1,1,512]{2,1,0:T(1,128)} %param.15) | copy-start | bytes 6148
  5.3 12.5 %copy-start.14 = (s32[1,1,512]{2,1,0:T(1,128)S(1)}, s32[1,1,512]{2,1,0:T(1,128)}, u32[]{:S(2)}) copy-start(s32[1,1,512]{2,1,0:T(1,128)} %param.14) | copy-start | bytes 6148
  5.3 12.5 %copy-start.6 = (s32[1,1,27,512]{3,1,2,0:T(1,128)S(1)}, s32[1,1,27,512]{3,1,2,0:T(1,128)}, u32[]{:S(2)}) copy-start(s32[1,1,27,512]{3,1,2,0:T(1,128)} %param.13) | copy-start | bytes 165892
  10.5 9.3 collective-permute-start
  16.4 8.3 collective-permute-start.1
  62.7 9.9 copy-start.5
  66.6 14.4 %all-to-all-start = ((f32[3,16,640]{2,0,1:T(4,128)}), f32[3,16,640]{2,0,1:T(4,128)S(1)}, u32[]{:S(2)}, u32[]{:S(2)}) async-start(f32[3,16,640]{2,0,1:T(4,128)} %bitcast.14), calls=%async_computation | async-start | bytes 327680 | tf_op jit(solution)/shard_map/all_to_all | solution.py:126
  72.6 11.5 copy-start.4
  181.8 5.0 copy-start.3
  287.8 8.1 collective-permute-start.2
  293.0 7.9 collective-permute-start.3
  343.2 12.6 %all-to-all-start.1 = ((f32[3,16,640]{2,0,1:T(4,128)}), f32[3,16,640]{2,0,1:T(4,128)}, u32[]{:S(2)}, u32[]{:S(2)}) async-start(f32[3,16,640]{2,0,1:T(4,128)} %bitcast.217), calls=%async_computation.1 | async-start | bytes 327680 | tf_op jit(solution)/shard_map/all_to_all | solution.py:126
  472.1 1.6 copy-start.2
  472.1 1.6 copy-start.11
  578.3 8.4 collective-permute-start.4
  583.9 9.0 collective-permute-start.5
  862.3 3.6 copy-start.12
  864.2 1.6 copy-start.1
  966.0 8.8 collective-permute-start.6
  971.7 9.1 collective-permute-start.7
  1163.7 3.3 copy-start
  (1 other events, 0.7 us)
where the time goes:
time: 1170 us
  other arithmetic  634 us (54%)
  local copies, waits for them, and re-layouts  318 us (27%)
  blocking collectives  143 us (12%)
  starting transfers between devices  36.9 us (3%)
  waiting for transfers between devices  22.3 us (2%)
    scatter-add x4, other arithmetic, assemble(): total_field = summed.at[:, peer_rows].add(arrived)  289 us
    scatter-add x3, other arithmetic, accumulate(): return summed_force.at[:, connect].add(contribution)  263 us
    gather x8, local copies, waits for them, and re-layouts, assemble(): summed[:, peer_rows]  156 us
    psum x3, blocking collectives, single_product(): lax.psum(jnp.sum(owner_weight * first_field * second_field), ('grp', 'dom'))  119 us
    gather x4, local copies, waits for them, and re-layouts, accumulate(): probe_field[:, connect]  66.9 us
    scatter-add x8, other arithmetic, assemble(): field.at[:, lower_ids].add(from_below).at[:, upper_ids].add(from_above)  39.9 us
    gather x2, local copies, waits for them, and re-layouts, accumulate(): state_field[:, connect]  31.1 us
    ppermute x8, starting transfers between devices, from_behind(): lax.ppermute(value, axis, [(source, source + steps) for source in range(l...  26.8 us
  transfers between devices with their start and end apart: 10, of which 8 were waited for; matrix products, arithmetic and copies ran while one was open for 2% of the time, Pallas kernels for 0%

commit v1 on v0

v1 whole, which is shorter than its diff:
```python
import functools
import math

import jax
import jax.numpy as jnp
import numpy as np
from jax import lax
from jax.experimental import pallas as pl
from jax.experimental.pallas import tpu as pltpu
from jax.sharding import PartitionSpec as P

MESH = pl.DeviceIdType.MESH
PZ = 8
LANES = 128
Q = 32
F32 = jnp.float32
BF16 = jnp.bfloat16
DIRECTIONS = (
    (0, -1, 640), (0, 1, 640), (-1, 0, 256), (1, 0, 256),
    (-1, -1, 128), (1, 1, 128), (-1, 1, 128), (1, -1, 128),
)
OPPOSITE = (1, 0, 3, 2, 5, 4, 7, 6)
STARTS = tuple(int(s) for s in np.cumsum([0] + [w for _, _, w in DIRECTIONS]))
DOM_WIDTH = STARTS[-1]


def lagrange_values(place):
    return np.array([place * (place - 1.0) / 2.0, 1.0 - place * place, place * (place + 1.0) / 2.0])


def lagrange_slopes(place):
    return np.array([place - 0.5, -2.0 * place, place + 0.5])


def basis_tables():
    points = [-math.sqrt(0.6), 0.0, math.sqrt(0.6)]
    weights = np.array([5.0 / 9.0, 8.0 / 9.0, 5.0 / 9.0])
    values = np.stack([lagrange_values(place) for place in points])
    slopes = np.stack([lagrange_slopes(place) for place in points])
    table = np.zeros((3, Q, Q))
    for d in range(3):
        factors = [slopes if d == k else values for k in range(3)]
        table[d, :27, :27] = np.einsum("ax,by,cz->abcxyz", *factors).reshape(27, 27)
    weight = np.einsum("a,b,c->abc", weights, weights, weights).reshape(27)
    forward = table.reshape(3 * Q, Q).copy()
    table[:, :27] *= weight[None, :, None]
    return forward, table.reshape(3 * Q, Q).T


def three_terms(table):
    table = np.asarray(table, np.float32)
    high = table.astype(BF16)
    low = (table - high.astype(np.float32)).astype(BF16)
    return jnp.asarray(np.concatenate([high, low, high], axis=1))


def halves(value):
    high = value.astype(BF16).astype(F32)
    return high, value - high


def stacked_halves(value):
    high, low = halves(value)
    return jnp.concatenate([high, low], axis=0).astype(BF16)


def one_hot(ids):
    spot = lax.broadcasted_iota(jnp.int32, (LANES, ids.shape[1]), 0)
    return jnp.where(spot == (ids & (LANES - 1)), 1.0, 0.0).astype(BF16)


def row_mask(ids, rows):
    spot = lax.broadcasted_iota(jnp.int32, (rows, ids.shape[1]), 0)
    return spot == (ids >> 7)


def pick(split_field, hot, ids):
    wide = jnp.dot(split_field, hot, preferred_element_type=F32)
    half = wide.shape[0] // 2
    wide = wide[:half] + wide[half:]
    rows = half // 3
    mask = row_mask(ids, rows)
    return [
        jnp.sum(jnp.where(mask, wide[c * rows : (c + 1) * rows], 0.0), axis=0, keepdims=True)
        for c in range(3)
    ]


def spread(values, hot, ids, rows):
    mask = row_mask(ids, rows)
    parts = [halves(value) for value in values]
    tall = jnp.concatenate([jnp.where(mask, parts[c][s], 0.0) for s in range(2) for c in range(3)], axis=0)
    total = lax.dot_general(
        tall.astype(BF16), hot, (((1,), (1,)), ((), ())), preferred_element_type=F32
    )
    return total


def cross(one, two):
    return [
        one[1] * two[2] - one[2] * two[1],
        one[2] * two[0] - one[0] * two[2],
        one[0] * two[1] - one[1] * two[0],
    ]


def kernel(
    n_grp, n_dom,
    conn, live, stiff, owner, free, faces, peers, disp, load, fwd, rev,
    update, residual,
    hot_e, hot_x, hot_d, ids_x, ids_d, nodal, inverse, coef, force,
    send_x, recv_x, send_d, recv_d, dot_send, dot_dom, dot_grp,
    sx, rx, sd, rd, s_dot, r_dot, s_grp, r_grp,
):
    grp, dom = lax.axis_index("grp"), lax.axis_index("dom")
    py, pz = dom // PZ, lax.rem(dom, PZ)
    n_py = n_dom // PZ
    rows = owner.shape[0]
    slots = conn.shape[1]

    def exists(way):
        sy, sz, _ = DIRECTIONS[way]
        return (py + sy >= 0) & (py + sy < n_py) & (pz + sz >= 0) & (pz + sz < PZ)

    def peer(way):
        sy, sz, _ = DIRECTIONS[way]
        return jnp.clip(dom + sy * PZ + sz, 0, n_dom - 1)

    recv_x[...] = jnp.zeros_like(recv_x)
    recv_d[...] = jnp.zeros_like(recv_d)
    send_x[...] = jnp.zeros_like(send_x)
    send_d[...] = jnp.zeros_like(send_d)

    barrier = pltpu.get_barrier_semaphore()
    for k in range(1, n_dom):
        pl.semaphore_signal(barrier, inc=1, device_id={"dom": lax.rem(dom + k, n_dom)}, device_id_type=MESH)
    for k in range(1, n_grp):
        pl.semaphore_signal(barrier, inc=1, device_id={"grp": lax.rem(grp + k, n_grp)}, device_id_type=MESH)

    width_x = faces.shape[1]
    for side in range(2):
        ids_x[:, side * width_x : (side + 1) * width_x] = faces[side : side + 1, :]
    for way, (_, _, width) in enumerate(DIRECTIONS):
        ids_d[:, STARTS[way] : STARTS[way + 1]] = peers[pl.ds(peer(way), 1), :][:, :width]
    hot_x[...] = one_hot(ids_x[...])
    hot_d[...] = one_hot(ids_d[...])

    @pl.loop(0, 27)
    def _(a):
        hot_e[a] = one_hot(conn[pl.ds(a, 1), :])

    nodal[...] = jnp.zeros_like(nodal)
    own = jnp.concatenate([owner[...].astype(F32)] * 3, axis=0)
    loose = jnp.concatenate([free[...].astype(F32)] * 3, axis=0)
    alive = live[...].astype(F32)
    shear = alive * stiff[...] / 2.6
    lame = alive * stiff[...] * 0.3 / 0.52

    pl.semaphore_wait(barrier, n_dom - 1 + n_grp - 1)

    def copy_x(turn, side):
        there = 1 - side
        return pltpu.make_async_remote_copy(
            src_ref=send_x.at[turn, :, pl.ds(side * width_x, width_x)],
            dst_ref=recv_x.at[turn, :, pl.ds(there * width_x, width_x)],
            send_sem=sx.at[turn, side],
            recv_sem=rx.at[turn, there],
            device_id={"grp": jnp.clip(grp + 2 * side - 1, 0, n_grp - 1)},
            device_id_type=MESH,
        )

    def copy_d(turn, way):
        there = OPPOSITE[way]
        width = DIRECTIONS[way][2]
        return pltpu.make_async_remote_copy(
            src_ref=send_d.at[turn, :, pl.ds(STARTS[way], width)],
            dst_ref=recv_d.at[turn, :, pl.ds(STARTS[there], width)],
            send_sem=sd.at[turn, way],
            recv_sem=rd.at[turn, there],
            device_id={"dom": peer(way)},
            device_id_type=MESH,
        )

    has_x = (grp > 0, grp < n_grp - 1)

    def added(total):
        half = total.shape[0] // 2
        return total[:half] + total[half:]

    def assemble(field, turn, between_x=None, between_d=None):
        picked = pick(stacked_halves(field), hot_x[...], ids_x[...])
        for c in range(3):
            send_x[turn, c : c + 1, :] = picked[c]
        for side in range(2):
            @pl.when(has_x[side])
            def _():
                copy_x(turn, side).start()
        if between_x is not None:
            between_x()
        for side in range(2):
            @pl.when(has_x[side])
            def _():
                copy_x(turn, side).wait_send()
                copy_x(turn, 1 - side).wait_recv()
        got = [recv_x[turn, c : c + 1, :] for c in range(3)]
        field = field + added(spread(got, hot_x[...], ids_x[...], rows))
        picked = pick(stacked_halves(field), hot_d[...], ids_d[...])
        for c in range(3):
            send_d[turn, c : c + 1, :] = picked[c]
        for way in range(8):
            @pl.when(exists(way))
            def _():
                copy_d(turn, way).start()
        if between_d is not None:
            between_d()
        for way in range(8):
            @pl.when(exists(way))
            def _():
                copy_d(turn, way).wait_send()
                copy_d(turn, OPPOSITE[way]).wait_recv()
        got = [recv_d[turn, c : c + 1, :] for c in range(3)]
        return field + added(spread(got, hot_d[...], ids_d[...], rows))

    def gradients(at):
        result = []
        for c in range(3):
            high, low = halves(nodal[c, :, at])
            stack = jnp.concatenate([high, high, low], axis=0).astype(BF16)
            full = jnp.dot(fwd[...], stack, preferred_element_type=F32)
            result.append([full[d * Q : (d + 1) * Q] for d in range(3)])
        return result

    def forces(field, tangent):
        split_field = stacked_halves(field)

        @pl.loop(0, 9)
        def _(step):
            for part in range(3):
                a = step * 3 + part
                picked = pick(split_field, hot_e[a], conn[pl.ds(a, 1), :])
                for c in range(3):
                    nodal[c, pl.ds(a, 1), :] = picked[c]

        for first in range(0, slots, LANES):
            at = slice(first, first + LANES)
            mu, lam = shear[:, at], lame[:, at]
            change = gradients(at)
            if tangent:
                inv = [[inverse[3 * i + j, :, at] for j in range(3)] for i in range(3)]
                twist = coef[:, at]
                product = [
                    [sum(inv[i][k] * change[k][j] for k in range(3)) for j in range(3)] for i in range(3)
                ]
                trace = lam * (product[0][0] + product[1][1] + product[2][2])
                stress = [
                    [
                        mu * change[c][d]
                        + twist * sum(product[d][k] * inv[k][c] for k in range(3))
                        + trace * inv[d][c]
                        for d in range(3)
                    ]
                    for c in range(3)
                ]
            else:
                deform = [[change[c][d] + (1.0 if c == d else 0.0) for d in range(3)] for c in range(3)]
                columns = [
                    cross(deform[1], deform[2]), cross(deform[2], deform[0]), cross(deform[0], deform[1])
                ]
                volume = sum(deform[0][i] * columns[0][i] for i in range(3))
                over = 1.0 / volume
                logged = lam * jnp.log(volume)
                twist = mu - logged
                coef[:, at] = twist
                inv = [[columns[j][i] * over for j in range(3)] for i in range(3)]
                for i in range(3):
                    for j in range(3):
                        inverse[3 * i + j, :, at] = inv[i][j]
                stress = [[mu * deform[c][d] - twist * inv[d][c] for d in range(3)] for c in range(3)]
            for c in range(3):
                tall = jnp.concatenate(stress[c], axis=0)
                high, low = halves(tall)
                stack = jnp.concatenate([high, high, low], axis=0).astype(BF16)
                force[c, :, at] = jnp.dot(rev[...], stack, preferred_element_type=F32)

        def body(step, total):
            for part in range(3):
                a = step * 3 + part
                values = [force[c, pl.ds(a, 1), :] for c in range(3)]
                total = total + spread(values, hot_e[a], conn[pl.ds(a, 1), :], rows)
            return total

        return added(lax.fori_loop(0, 9, body, jnp.zeros((6 * rows, LANES), F32)))

    state = assemble(own * disp[...], 0)
    inner = forces(state, False)
    right = loose * assemble(own * load[...] - inner, 1)
    image = loose * assemble(forces(right, True), 2)
    second = forces(image, True)

    def lanes(value):
        return jnp.sum(value, axis=0, keepdims=True)

    partial = [
        lanes(own * right * right), lanes(own * right * image),
        lanes(own * image * image), lanes(image * second),
    ]
    dot_send[0] = jnp.concatenate(partial + [jnp.zeros((4, LANES), F32)], axis=0)

    def dot_copy(k):
        return pltpu.make_async_remote_copy(
            src_ref=dot_send.at[0], dst_ref=dot_dom.at[k], send_sem=s_dot.at[k], recv_sem=r_dot.at[k],
            device_id={"dom": lax.rem(dom + k, n_dom)}, device_id_type=MESH,
        )

    def grp_copy(k):
        return pltpu.make_async_remote_copy(
            src_ref=dot_send.at[1], dst_ref=dot_grp.at[k], send_sem=s_grp.at[k], recv_sem=r_grp.at[k],
            device_id={"grp": lax.rem(grp + k, n_grp)}, device_id_type=MESH,
        )

    def start_dots():
        for k in range(1, n_dom):
            dot_copy(k).start()

    def middle_dots():
        total = dot_send[0]
        for k in range(1, n_dom):
            dot_copy(k).wait()
            total = total + dot_dom[k]
        dot_send[1] = total
        for k in range(1, n_grp):
            grp_copy(k).start()

    outer = loose * assemble(second, 3, start_dots, middle_dots)
    total = dot_send[1]
    for k in range(1, n_grp):
        grp_copy(k).wait()
        total = total + dot_grp[k]
    sums = jnp.sum(total, axis=1, keepdims=True)
    rr, rq, qq, qu = (sums[k : k + 1] for k in range(4))
    step = rr / rq
    later = step * step * qq - rr
    ratio = later / rr
    grown = 1.0 + ratio
    curve = grown * grown * rq - 2.0 * grown * step * qq + step * step * qu
    last = later / curve
    moved = right - step * image
    direction = moved + ratio * right
    update[...] = step * right + last * direction
    residual[...] = moved - last * (grown * image - step * outer)


def per_device(n_grp, n_dom, conn, live, stiffness, owner, free, x_faces, peer_table, disp, load):
    slots = conn.shape[3]
    rows = owner.shape[2] // LANES
    width_x = x_faces.shape[3]
    forward, backward = basis_tables()
    vmem = pl.BlockSpec(memory_space=pltpu.VMEM)
    shape = jax.ShapeDtypeStruct((3 * rows, LANES), F32)
    dma = pltpu.SemaphoreType.DMA
    update, residual = pl.pallas_call(
        functools.partial(kernel, n_grp, n_dom),
        out_shape=(shape, shape),
        in_specs=[vmem] * 11,
        out_specs=(vmem, vmem),
        scratch_shapes=[
            pltpu.VMEM((27, LANES, slots), BF16),
            pltpu.VMEM((LANES, 2 * width_x), BF16),
            pltpu.VMEM((LANES, DOM_WIDTH), BF16),
            pltpu.VMEM((1, 2 * width_x), jnp.int32),
            pltpu.VMEM((1, DOM_WIDTH), jnp.int32),
            pltpu.VMEM((3, Q, slots), F32),
            pltpu.VMEM((9, Q, slots), F32),
            pltpu.VMEM((Q, slots), F32),
            pltpu.VMEM((3, Q, slots), F32),
            pltpu.VMEM((4, 8, 2 * width_x), F32),
            pltpu.VMEM((4, 8, 2 * width_x), F32),
            pltpu.VMEM((4, 8, DOM_WIDTH), F32),
            pltpu.VMEM((4, 8, DOM_WIDTH), F32),
            pltpu.VMEM((2, 8, LANES), F32),
            pltpu.VMEM((n_dom, 8, LANES), F32),
            pltpu.VMEM((n_grp, 8, LANES), F32),
            dma((4, 2)), dma((4, 2)), dma((4, 8)), dma((4, 8)),
            dma((n_dom,)), dma((n_dom,)), dma((n_grp,)), dma((n_grp,)),
        ],
        compiler_params=pltpu.CompilerParams(
            collective_id=0, has_side_effects=True, vmem_limit_bytes=48 * 1024 * 1024
        ),
        cost_estimate=pl.CostEstimate(flops=4 * 10**9, bytes_accessed=10**6, transcendentals=10**4),
    )(
        conn[0, 0], live[0], stiffness[0],
        owner.reshape(rows, LANES), free.reshape(rows, LANES),
        x_faces[0, 0], peer_table[0],
        disp.reshape(3 * rows, LANES), load.reshape(3 * rows, LANES),
        three_terms(forward), three_terms(backward),
    )
    return update.reshape(disp.shape), residual.reshape(disp.shape)


def solution(mesh):
    field = P("grp", "dom", None, None)
    flat = P("grp", "dom", None)
    in_specs = (field, flat, flat, flat, flat, field, flat, field, field)
    return jax.shard_map(
        functools.partial(per_device, mesh.shape["grp"], mesh.shape["dom"]),
        mesh=mesh, in_specs=in_specs, out_specs=(field, field), check_vma=False,
    )
```

time: 1170 us -> 68.3 us (0.06)
  other arithmetic: 634 us -> 0 us
  local copies, waits for them, and re-layouts: 318 us -> 5.84 us
  blocking collectives: 143 us -> 0 us
  Pallas kernels: 0 us -> 61.3 us
  starting transfers between devices: 36.9 us -> 0 us
  waiting for transfers between devices: 22.3 us -> 0 us
    scatter-add x15 -> x0, other arithmetic: 591 us -> none  [the longest x4 289 us: assemble(): total_field = summed.at[:, peer_rows].add(arrived)]
    gather x22 -> x0, local copies, waits for them, and re-layouts: 272 us -> none  [the longest x8 156 us: assemble(): summed[:, peer_rows]]
    psum x3 -> x0, blocking collectives: 119 us -> none  [single_product(): lax.psum(jnp.sum(owner_weight * first_field * second_field), ('grp', 'dom'))]
    pallas_call x0 -> x1, Pallas kernels: none -> 61.3 us  [per_device(): pl.pallas_call(functools.partial(kernel, n_grp, n_dom), out_shape=(shape,...]
    ppermute x8 -> x0, starting transfers between devices: 26.8 us -> none  [from_behind(): lax.ppermute(value, axis, [(source, source + steps) for source in range(l...]
    all_to_all x2 -> x0, blocking collectives: 23.9 us -> none  [assemble(): lax.all_to_all(summed[:, peer_rows], 'dom', split_axis=1, concat_axis=1,...]
    reduce_sum x7 -> x0, other arithmetic: 18.1 us -> none  [the longest x3 15 us: single_product(): jnp.sum(owner_weight * first_field * second_field)]
    all_to_all x4 -> x0, local copies, waits for them, and re-layouts: 14.2 us -> none  [assemble(): lax.all_to_all(summed[:, peer_rows], 'dom', split_axis=1, concat_axis=1,...]
  transfers between devices with their start and end apart: 10 -> 0, of which waited for: 8 -> 0; matrix products, arithmetic and copies ran while one was open for 2% -> 0% of each run, Pallas kernels for 0% -> 0%
where the time goes in v1:
time: 68.3 us; the launch traced here: 67.8 us
  Pallas kernels  61.3 us (90%)
  local copies, waits for them, and re-layouts  5.84 us (9%)
  between operations  0.72 us (1%)
    pallas_call x1, Pallas kernels, per_device(): pl.pallas_call(functools.partial(kernel, n_grp, n_dom), out_shape=(shape,...  61.3 us
    unnamed x23, local copies, waits for them, and re-layouts  5.84 us

profile of v1, /device:TPU:0, one launch (start us, length us, event | category | flops | bytes accessed | tf_op | source)
XLA Modules:
  0.0 67.8 jit_solution(8676118804332252030)
XLA Ops:
  0.6 0.0 copy-start.7
  0.6 0.0 copy-start.6
  0.7 0.0 copy-start.5
  0.7 0.0 copy-start.1
  0.7 0.0 copy-start
  0.7 0.9 %copy.19 = s32[1,1,27,512]{3,2,1,0:T(8,128)S(1)} copy(s32[1,1,27,512]{3,1,2,0:T(1,128)} %param.11) | data formatting | bytes 110592
  1.5 0.0 copy-done.7
  1.5 0.0 copy-done.6
  1.6 0.0 copy-done.5
  1.6 0.0 copy-done.1
  1.6 0.0 copy-done
  1.6 0.0 copy-start.2
  1.6 0.8 %copy-done.2 = s32[1,16,640]{2,1,0:T(8,128)S(1)} copy-done((s32[1,16,640]{2,1,0:T(8,128)S(1)}, s32[1,16,640]{2,1,0:T(8,128)}, u32[]{:S(2)}) %copy-start.2) | copy-done | bytes 40984
  2.4 0.0 copy-start.3
  2.4 0.7 %copy-done.3 = s32[1,1,5120]{2,1,0:T(1,128)S(1)} copy-done((s32[1,1,5120]{2,1,0:T(1,128)S(1)}, s32[1,1,5120]{2,1,0:T(1,128)}, u32[]{:S(2)}) %copy-start.3) | copy-done | bytes 20504
  3.1 0.0 copy-start.4
  3.1 0.7 %copy-done.4 = s32[1,1,5120]{2,1,0:T(1,128)S(1)} copy-done((s32[1,1,5120]{2,1,0:T(1,128)S(1)}, s32[1,1,5120]{2,1,0:T(1,128)}, u32[]{:S(2)}) %copy-start.4) | copy-done | bytes 20504
  3.8 0.0 copy-start.8
  3.8 0.7 %copy-done.8 = bf16[32,288]{1,0:T(8,128)(2,1)S(1)} copy-done((bf16[32,288]{1,0:T(8,128)(2,1)S(1)}, bf16[32,288]{1,0:T(8,128)(2,1)}, u32[]{:S(2)}) %copy-start.8) | copy-done | bytes 18456
  4.6 0.0 copy-start.9
  4.6 0.7 %copy-done.9 = bf16[96,96]{1,0:T(8,128)(2,1)S(1)} copy-done((bf16[96,96]{1,0:T(8,128)(2,1)S(1)}, bf16[96,96]{1,0:T(8,128)(2,1)}, u32[]{:S(2)}) %copy-start.9) | copy-done | bytes 18456
  5.3 61.3 %shard_map.122 = (f32[120,128]{1,0:T(8,128)S(1)}, f32[120,128]{1,0:T(8,128)S(1)}) custom-call(s32[27,512]{1,0:T(8,128)S(1)} %bitcast.13, s32[1,512]{1,0:T(1,128)S(1)} %bitcast.22, f32[1,512]{1,0:T(1,128)S(1)} %bitcast.23, s32[40,128]{1,0:T(8,128)S(1)} %bitcast.19, s32[40,128]{1,0:T(8,128)S(1)} %bitcast.20, s32[2,384]{1,0:T(2,128)S(1)} %bitcast.21, ...), custom_call_target="tpu_custom_call" | custom-call | flops 4000000000 | bytes 1000000 | tf_op jit(solution)/shard_map/pallas_call | solution.py:361
  66.6 0.6 copy.22
  67.2 0.6 copy.23
Async XLA Ops:
  0.6 0.9 %copy-start.7 = (f32[1,1,512]{2,1,0:T(1,128)S(1)}, f32[1,1,512]{2,1,0:T(1,128)}, u32[]{:S(2)}) copy-start(f32[1,1,512]{2,1,0:T(1,128)} %param.13) | copy-start | bytes 6148
  0.6 0.9 %copy-start.6 = (s32[1,1,512]{2,1,0:T(1,128)S(1)}, s32[1,1,512]{2,1,0:T(1,128)}, u32[]{:S(2)}) copy-start(s32[1,1,512]{2,1,0:T(1,128)} %param.12) | copy-start | bytes 6148
  0.7 0.9 %copy-start.5 = (s32[1,1,2,384]{3,2,1,0:T(2,128)S(1)}, s32[1,1,2,384]{3,2,1,0:T(2,128)}, u32[]{:S(2)}) copy-start(s32[1,1,2,384]{3,2,1,0:T(2,128)} %param.16) | copy-start | bytes 9220
  0.7 0.9 %copy-start.1 = (f32[1,1,3,5120]{3,1,2,0:T(1,128)S(1)}, f32[1,1,3,5120]{3,1,2,0:T(1,128)}, u32[]{:S(2)}) copy-start(f32[1,1,3,5120]{3,1,2,0:T(1,128)} %param.19) | copy-start | bytes 184324
  0.7 0.9 %copy-start = (f32[1,1,3,5120]{3,1,2,0:T(1,128)S(1)}, f32[1,1,3,5120]{3,1,2,0:T(1,128)}, u32[]{:S(2)}) copy-start(f32[1,1,3,5120]{3,1,2,0:T(1,128)} %param.18) | copy-start | bytes 184324
  1.6 0.8 %copy-start.2 = (s32[1,16,640]{2,1,0:T(8,128)S(1)}, s32[1,16,640]{2,1,0:T(8,128)}, u32[]{:S(2)}) copy-start(s32[1,16,640]{2,1,0:T(8,128)} %param.17) | copy-start | bytes 122884
  2.4 0.7 %copy-start.3 = (s32[1,1,5120]{2,1,0:T(1,128)S(1)}, s32[1,1,5120]{2,1,0:T(1,128)}, u32[]{:S(2)}) copy-start(s32[1,1,5120]{2,1,0:T(1,128)} %param.14) | copy-start | bytes 61444
  3.1 0.7 %copy-start.4 = (s32[1,1,5120]{2,1,0:T(1,128)S(1)}, s32[1,1,5120]{2,1,0:T(1,128)}, u32[]{:S(2)}) copy-start(s32[1,1,5120]{2,1,0:T(1,128)} %param.15) | copy-start | bytes 61444
  3.8 0.7 %copy-start.8 = (bf16[32,288]{1,0:T(8,128)(2,1)S(1)}, bf16[32,288]{1,0:T(8,128)(2,1)}, u32[]{:S(2)}) copy-start(bf16[32,288]{1,0:T(8,128)(2,1)} %constant.5.clone.rev) | copy-start | bytes 55300
  4.6 0.7 %copy-start.9 = (bf16[96,96]{1,0:T(8,128)(2,1)S(1)}, bf16[96,96]{1,0:T(8,128)(2,1)}, u32[]{:S(2)}) copy-start(bf16[96,96]{1,0:T(8,128)(2,1)} %constant.4.clone.fwd) | copy-start | bytes 55300

commit v2 on v1

--- a/solution.py
+++ b/solution.py
@@ -11,7 +11,9 @@
 
 MESH = pl.DeviceIdType.MESH
 PZ = 8
-LANES = 128
+LANES = 256
+CHUNK = 128
+UNROLL = 9
 Q = 32
 F32 = jnp.float32
 BF16 = jnp.bfloat16
@@ -71,7 +73,7 @@
 
 def row_mask(ids, rows):
     spot = lax.broadcasted_iota(jnp.int32, (rows, ids.shape[1]), 0)
-    return spot == (ids >> 7)
+    return spot == (ids >> 8)
 
 
 def pick(split_field, hot, ids):
@@ -108,14 +110,15 @@
     n_grp, n_dom,
     conn, live, stiff, owner, free, faces, peers, disp, load, fwd, rev,
     update, residual,
-    hot_e, hot_x, hot_d, ids_x, ids_d, nodal, inverse, coef, force,
+    padded, hot_e, hot_x, hot_d, ids_x, ids_d, nodal, inverse, coef, force,
     send_x, recv_x, send_d, recv_d, dot_send, dot_dom, dot_grp,
     sx, rx, sd, rd, s_dot, r_dot, s_grp, r_grp,
 ):
     grp, dom = lax.axis_index("grp"), lax.axis_index("dom")
     py, pz = dom // PZ, lax.rem(dom, PZ)
     n_py = n_dom // PZ
-    rows = owner.shape[0]
+    kept = owner.shape[0]
+    rows = padded.shape[1] // 3
     slots = conn.shape[1]
 
     def exists(way):
@@ -150,8 +153,14 @@
         hot_e[a] = one_hot(conn[pl.ds(a, 1), :])
 
     nodal[...] = jnp.zeros_like(nodal)
-    own = jnp.concatenate([owner[...].astype(F32)] * 3, axis=0)
-    loose = jnp.concatenate([free[...].astype(F32)] * 3, axis=0)
+    padded[...] = jnp.zeros_like(padded)
+    for c in range(3):
+        here, there = pl.ds(c * kept, kept), pl.ds(c * rows, kept)
+        padded[0, there, :] = owner[...].astype(F32)
+        padded[1, there, :] = free[...].astype(F32)
+        padded[2, there, :] = disp[here, :]
+        padded[3, there, :] = load[here, :]
+    own, loose = padded[0], padded[1]
     alive = live[...].astype(F32)
     shear = alive * stiff[...] / 2.6
     lame = alive * stiff[...] * 0.3 / 0.52
@@ -233,16 +242,16 @@
     def forces(field, tangent):
         split_field = stacked_halves(field)
 
-        @pl.loop(0, 9)
+        @pl.loop(0, 27 // UNROLL)
         def _(step):
-            for part in range(3):
-                a = step * 3 + part
+            for part in range(UNROLL):
+                a = step * UNROLL + part
                 picked = pick(split_field, hot_e[a], conn[pl.ds(a, 1), :])
                 for c in range(3):
                     nodal[c, pl.ds(a, 1), :] = picked[c]
 
-        for first in range(0, slots, LANES):
-            at = slice(first, first + LANES)
+        for first in range(0, slots, CHUNK):
+            at = slice(first, first + CHUNK)
             mu, lam = shear[:, at], lame[:, at]
             change = gradients(at)
             if tangent:
@@ -283,17 +292,17 @@
                 force[c, :, at] = jnp.dot(rev[...], stack, preferred_element_type=F32)
 
         def body(step, total):
-            for part in range(3):
-                a = step * 3 + part
+            for part in range(UNROLL):
+                a = step * UNROLL + part
                 values = [force[c, pl.ds(a, 1), :] for c in range(3)]
                 total = total + spread(values, hot_e[a], conn[pl.ds(a, 1), :], rows)
             return total
 
-        return added(lax.fori_loop(0, 9, body, jnp.zeros((6 * rows, LANES), F32)))
-
-    state = assemble(own * disp[...], 0)
+        return added(lax.fori_loop(0, 27 // UNROLL, body, jnp.zeros((6 * rows, LANES), F32)))
+
+    state = assemble(own * padded[2], 0)
     inner = forces(state, False)
-    right = loose * assemble(own * load[...] - inner, 1)
+    right = loose * assemble(own * padded[3] - inner, 1)
     image = loose * assemble(forces(right, True), 2)
     second = forces(image, True)
 
@@ -346,8 +355,12 @@
     last = later / curve
     moved = right - step * image
     direction = moved + ratio * right
-    update[...] = step * right + last * direction
-    residual[...] = moved - last * (grown * image - step * outer)
+    padded[2] = step * right + last * direction
+    padded[3] = moved - last * (grown * image - step * outer)
+    for c in range(3):
+        here, there = pl.ds(c * kept, kept), pl.ds(c * rows, kept)
+        update[here, :] = padded[2, there, :]
+        residual[here, :] = padded[3, there, :]
 
 
 def per_device(n_grp, n_dom, conn, live, stiffness, owner, free, x_faces, peer_table, disp, load):
@@ -364,6 +377,7 @@
         in_specs=[vmem] * 11,
         out_specs=(vmem, vmem),
         scratch_shapes=[
+            pltpu.VMEM((4, 3 * (-(-rows // 8) * 8), LANES), F32),
             pltpu.VMEM((27, LANES, slots), BF16),
             pltpu.VMEM((LANES, 2 * width_x), BF16),
             pltpu.VMEM((LANES, DOM_WIDTH), BF16),

time: 68.3 us -> 62.2 us (0.911)
  Pallas kernels: 61.3 us -> 54.1 us
  other arithmetic: 0 us -> 2.45 us
  local copies, waits for them, and re-layouts: 5.84 us -> 4.38 us
    pallas_call x1, Pallas kernels: 61.3 us -> 54.1 us  [per_device(): pl.pallas_call(functools.partial(kernel, n_grp, n_dom), out_shape=(shape,...]
    unnamed x23 -> x22, local copies, waits for them, and re-layouts: 5.84 us -> 2.91 us
    unnamed x0 -> x4, other arithmetic: none -> 2.45 us
    reshape x0 -> x6, local copies, waits for them, and re-layouts: none -> 1.48 us  [the longest x2 1.37 us: per_device(): return (update.reshape(disp.shape), residual.reshape(disp.shape))]
where the time goes in v2:
time: 62.2 us; the launch traced here: 61.7 us
  Pallas kernels  54.1 us (87%)
  local copies, waits for them, and re-layouts  4.38 us (7%)
  other arithmetic  2.45 us (4%)
  between operations  0.76 us (1%)
    pallas_call x1, Pallas kernels, per_device(): pl.pallas_call(functools.partial(kernel, n_grp, n_dom), out_shape=(shape,...  54.1 us
    unnamed x22, local copies, waits for them, and re-layouts  2.91 us
    unnamed x4, other arithmetic  2.45 us
    reshape x2, local copies, waits for them, and re-layouts, per_device(): return (update.reshape(disp.shape), residual.reshape(disp.shape))  1.37 us

profile of v2, /device:TPU:0, one launch (start us, length us, event | category | flops | bytes accessed | tf_op | source)
XLA Modules:
  0.0 61.7 jit_solution(7012919879803750768)
XLA Ops:
  0.6 0.5 broadcast.8
  1.1 1.4 %reduce.8 = s32[5120]{0:T(1024)S(1)} reduce(s32[1,1,5120]{2,1,0:T(1,128)} %param.14, s32[]{:T(128)} %broadcast.8), dimensions={0,1}, to_apply=%param.14.reduce_sub_computation.3 | reduce | bytes 40964 | tf_op args[3]
  2.6 0.0 copy-start.8
  2.6 0.0 copy-done.9
  2.6 0.7 %reduce.9 = s32[5120]{0:T(1024)S(1)} reduce(s32[1,1,5120]{2,1,0:T(1,128)S(1)} %copy-done.9, s32[]{:T(128)} %broadcast.8), dimensions={0,1}, to_apply=%param.15.reduce_sub_computation.3 | reduce | bytes 40964 | tf_op args[4]
  3.3 0.1 copy-done.8
  3.4 0.8 %copy-done.6 = f32[1,1,3,5120]{3,1,2,0:T(1,128)S(1)} copy-done((f32[1,1,3,5120]{3,1,2,0:T(1,128)S(1)}, f32[1,1,3,5120]{3,1,2,0:T(1,128)}, u32[]{:S(2)}) %copy-start.6) | copy-done | bytes 61464
  4.2 0.2 reduce.2
  4.4 0.0 copy-start.7
  4.5 0.8 %copy-done.7 = f32[1,1,3,5120]{3,1,2,0:T(1,128)S(1)} copy-done((f32[1,1,3,5120]{3,1,2,0:T(1,128)S(1)}, f32[1,1,3,5120]{3,1,2,0:T(1,128)}, u32[]{:S(2)}) %copy-start.7) | copy-done | bytes 61464
  5.2 0.2 reduce.3
  5.4 0.0 copy-start
  5.4 0.0 copy-start.1
  5.4 0.0 copy-start.2
  5.4 0.0 copy-start.3
  5.4 0.0 copy-start.4
  5.4 0.0 copy-start.5
  5.5 0.7 %copy-done = s32[1,16,640]{2,1,0:T(8,128)S(1)} copy-done((s32[1,16,640]{2,1,0:T(8,128)S(1)}, s32[1,16,640]{2,1,0:T(8,128)}, u32[]{:S(2)}) %copy-start) | copy-done | bytes 40984
  6.2 0.0 copy-done.1
  6.2 0.0 copy-done.4
  6.2 0.0 copy-done.5
  6.2 54.1 %shard_map.122 = (f32[60,256]{1,0:T(8,128)S(1)}, f32[60,256]{1,0:T(8,128)S(1)}) custom-call(s32[27,512]{1,0:T(8,128)S(1)} %bitcast.7, s32[1,512]{1,0:T(1,128)S(1)} %bitcast.10, f32[1,512]{1,0:T(1,128)S(1)} %bitcast.11, s32[20,256]{1,0:T(8,128)S(1)} %reshape.22.owner, s32[20,256]{1,0:T(8,128)S(1)} %reshape.23.free, s32[2,384]{1,0:T(2,128)S(1)} %bitcast.9, ...), custom_call_target="tpu_custom_call" | custom-call | flops 4000000000 | bytes 1000000 | tf_op jit(solution)/shard_map/pallas_call | solution.py:374
  60.4 0.7 %reshape.28 = f32[1,1,3,5120]{3,1,2,0:T(1,128)} reshape(f32[60,256]{1,0:T(8,128)S(1)} %get-tuple-element.4) | data formatting | bytes 122880 | tf_op jit(solution)/shard_map/reshape | solution.py:411
  61.0 0.7 %reshape.29 = f32[1,1,3,5120]{3,1,2,0:T(1,128)} reshape(f32[60,256]{1,0:T(8,128)S(1)} %get-tuple-element.5) | data formatting | bytes 122880 | tf_op jit(solution)/shard_map/reshape | solution.py:411
  (9 shorter events, 0.1 us)
Async XLA Ops:
  1.1 1.5 %copy-start.9 = (s32[1,1,5120]{2,1,0:T(1,128)S(1)}, s32[1,1,5120]{2,1,0:T(1,128)}, u32[]{:S(2)}) copy-start(s32[1,1,5120]{2,1,0:T(1,128)} %param.15) | copy-start | bytes 61444
  2.6 0.8 %copy-start.8 = (s32[1,1,27,512]{3,1,2,0:T(1,128)S(1)}, s32[1,1,27,512]{3,1,2,0:T(1,128)}, u32[]{:S(2)}) copy-start(s32[1,1,27,512]{3,1,2,0:T(1,128)} %param.11) | copy-start | bytes 165892
  3.4 0.8 %copy-start.6 = (f32[1,1,3,5120]{3,1,2,0:T(1,128)S(1)}, f32[1,1,3,5120]{3,1,2,0:T(1,128)}, u32[]{:S(2)}) copy-start(f32[1,1,3,5120]{3,1,2,0:T(1,128)} %param.18) | copy-start | bytes 184324
  4.4 0.8 %copy-start.7 = (f32[1,1,3,5120]{3,1,2,0:T(1,128)S(1)}, f32[1,1,3,5120]{3,1,2,0:T(1,128)}, u32[]{:S(2)}) copy-start(f32[1,1,3,5120]{3,1,2,0:T(1,128)} %param.19) | copy-start | bytes 184324
  5.4 0.8 %copy-start = (s32[1,16,640]{2,1,0:T(8,128)S(1)}, s32[1,16,640]{2,1,0:T(8,128)}, u32[]{:S(2)}) copy-start(s32[1,16,640]{2,1,0:T(8,128)} %param.17) | copy-start | bytes 122884
  5.4 0.8 %copy-start.1 = (s32[1,1,2,384]{3,2,1,0:T(2,128)S(1)}, s32[1,1,2,384]{3,2,1,0:T(2,128)}, u32[]{:S(2)}) copy-start(s32[1,1,2,384]{3,2,1,0:T(2,128)} %param.16) | copy-start | bytes 9220
  5.4 0.8 %copy-start.2 = (s32[1,1,512]{2,1,0:T(1,128)S(1)}, s32[1,1,512]{2,1,0:T(1,128)}, u32[]{:S(2)}) copy-start(s32[1,1,512]{2,1,0:T(1,128)} %param.12) | copy-start | bytes 6148
  5.4 0.8 %copy-start.3 = (f32[1,1,512]{2,1,0:T(1,128)S(1)}, f32[1,1,512]{2,1,0:T(1,128)}, u32[]{:S(2)}) copy-start(f32[1,1,512]{2,1,0:T(1,128)} %param.13) | copy-start | bytes 6148
  5.4 0.8 %copy-start.4 = (bf16[32,288]{1,0:T(8,128)(2,1)S(1)}, bf16[32,288]{1,0:T(8,128)(2,1)}, u32[]{:S(2)}) copy-start(bf16[32,288]{1,0:T(8,128)(2,1)} %constant.5.clone.rev) | copy-start | bytes 55300
  5.4 0.8 %copy-start.5 = (bf16[96,96]{1,0:T(8,128)(2,1)S(1)}, bf16[96,96]{1,0:T(8,128)(2,1)}, u32[]{:S(2)}) copy-start(bf16[96,96]{1,0:T(8,128)(2,1)} %constant.4.clone.fwd) | copy-start | bytes 55300

commit v3 on v2

--- a/solution.py
+++ b/solution.py
@@ -13,7 +13,8 @@
 PZ = 8
 LANES = 256
 CHUNK = 128
-UNROLL = 9
+GATHER_UNROLL = 27
+SCATTER_UNROLL = 9
 Q = 32
 F32 = jnp.float32
 BF16 = jnp.bfloat16
@@ -242,10 +243,10 @@
     def forces(field, tangent):
         split_field = stacked_halves(field)
 
-        @pl.loop(0, 27 // UNROLL)
+        @pl.loop(0, 27 // GATHER_UNROLL)
         def _(step):
-            for part in range(UNROLL):
-                a = step * UNROLL + part
+            for part in range(GATHER_UNROLL):
+                a = step * GATHER_UNROLL + part
                 picked = pick(split_field, hot_e[a], conn[pl.ds(a, 1), :])
                 for c in range(3):
                     nodal[c, pl.ds(a, 1), :] = picked[c]
@@ -292,13 +293,13 @@
                 force[c, :, at] = jnp.dot(rev[...], stack, preferred_element_type=F32)
 
         def body(step, total):
-            for part in range(UNROLL):
-                a = step * UNROLL + part
+            for part in range(SCATTER_UNROLL):
+                a = step * SCATTER_UNROLL + part
                 values = [force[c, pl.ds(a, 1), :] for c in range(3)]
                 total = total + spread(values, hot_e[a], conn[pl.ds(a, 1), :], rows)
             return total
 
-        return added(lax.fori_loop(0, 27 // UNROLL, body, jnp.zeros((6 * rows, LANES), F32)))
+        return added(lax.fori_loop(0, 27 // SCATTER_UNROLL, body, jnp.zeros((6 * rows, LANES), F32)))
 
     state = assemble(own * padded[2], 0)
     inner = forces(state, False)

time: 62.2 us -> 61.8 us (level)
  no operation moved by 1% of the time
where the time goes in v3:
time: 61.8 us; the launch traced here: 61.4 us
  Pallas kernels  53.8 us (87%)
  local copies, waits for them, and re-layouts  4.38 us (7%)
  other arithmetic  2.45 us (4%)
  between operations  0.76 us (1%)
    pallas_call x1, Pallas kernels, per_device(): pl.pallas_call(functools.partial(kernel, n_grp, n_dom), out_shape=(shape,...  53.8 us
    unnamed x22, local copies, waits for them, and re-layouts  2.91 us
    unnamed x4, other arithmetic  2.45 us
    reshape x2, local copies, waits for them, and re-layouts, per_device(): return (update.reshape(disp.shape), residual.reshape(disp.shape))  1.37 us

profile of v3, /device:TPU:0, one launch (start us, length us, event | category | flops | bytes accessed | tf_op | source)
XLA Modules:
  0.0 61.4 jit_solution(7782146795495467025)
XLA Ops:
  0.6 0.5 broadcast.8
  1.1 1.4 %reduce.8 = s32[5120]{0:T(1024)S(1)} reduce(s32[1,1,5120]{2,1,0:T(1,128)} %param.14, s32[]{:T(128)} %broadcast.8), dimensions={0,1}, to_apply=%param.14.reduce_sub_computation.3 | reduce | bytes 40964 | tf_op args[3]
  2.6 0.0 copy-start.8
  2.6 0.0 copy-done.9
  2.6 0.7 %reduce.9 = s32[5120]{0:T(1024)S(1)} reduce(s32[1,1,5120]{2,1,0:T(1,128)S(1)} %copy-done.9, s32[]{:T(128)} %broadcast.8), dimensions={0,1}, to_apply=%param.15.reduce_sub_computation.3 | reduce | bytes 40964 | tf_op args[4]
  3.3 0.1 copy-done.8
  3.4 0.8 %copy-done.6 = f32[1,1,3,5120]{3,1,2,0:T(1,128)S(1)} copy-done((f32[1,1,3,5120]{3,1,2,0:T(1,128)S(1)}, f32[1,1,3,5120]{3,1,2,0:T(1,128)}, u32[]{:S(2)}) %copy-start.6) | copy-done | bytes 61464
  4.2 0.2 reduce.2
  4.4 0.0 copy-start.7
  4.5 0.8 %copy-done.7 = f32[1,1,3,5120]{3,1,2,0:T(1,128)S(1)} copy-done((f32[1,1,3,5120]{3,1,2,0:T(1,128)S(1)}, f32[1,1,3,5120]{3,1,2,0:T(1,128)}, u32[]{:S(2)}) %copy-start.7) | copy-done | bytes 61464
  5.2 0.2 reduce.3
  5.4 0.0 copy-start
  5.4 0.0 copy-start.1
  5.4 0.0 copy-start.2
  5.4 0.0 copy-start.3
  5.4 0.0 copy-start.4
  5.4 0.0 copy-start.5
  5.5 0.7 %copy-done = s32[1,16,640]{2,1,0:T(8,128)S(1)} copy-done((s32[1,16,640]{2,1,0:T(8,128)S(1)}, s32[1,16,640]{2,1,0:T(8,128)}, u32[]{:S(2)}) %copy-start) | copy-done | bytes 40984
  6.2 0.0 copy-done.1
  6.2 0.0 copy-done.4
  6.2 0.0 copy-done.5
  6.2 53.8 %shard_map.122 = (f32[60,256]{1,0:T(8,128)S(1)}, f32[60,256]{1,0:T(8,128)S(1)}) custom-call(s32[27,512]{1,0:T(8,128)S(1)} %bitcast.7, s32[1,512]{1,0:T(1,128)S(1)} %bitcast.10, f32[1,512]{1,0:T(1,128)S(1)} %bitcast.11, s32[20,256]{1,0:T(8,128)S(1)} %reshape.22.owner, s32[20,256]{1,0:T(8,128)S(1)} %reshape.23.free, s32[2,384]{1,0:T(2,128)S(1)} %bitcast.9, ...), custom_call_target="tpu_custom_call" | custom-call | flops 4000000000 | bytes 1000000 | tf_op jit(solution)/shard_map/pallas_call | solution.py:375
  60.0 0.7 %reshape.28 = f32[1,1,3,5120]{3,1,2,0:T(1,128)} reshape(f32[60,256]{1,0:T(8,128)S(1)} %get-tuple-element.4) | data formatting | bytes 122880 | tf_op jit(solution)/shard_map/reshape | solution.py:412
  60.7 0.7 %reshape.29 = f32[1,1,3,5120]{3,1,2,0:T(1,128)} reshape(f32[60,256]{1,0:T(8,128)S(1)} %get-tuple-element.5) | data formatting | bytes 122880 | tf_op jit(solution)/shard_map/reshape | solution.py:412
  (9 shorter events, 0.1 us)
Async XLA Ops:
  1.1 1.5 %copy-start.9 = (s32[1,1,5120]{2,1,0:T(1,128)S(1)}, s32[1,1,5120]{2,1,0:T(1,128)}, u32[]{:S(2)}) copy-start(s32[1,1,5120]{2,1,0:T(1,128)} %param.15) | copy-start | bytes 61444
  2.6 0.8 %copy-start.8 = (s32[1,1,27,512]{3,1,2,0:T(1,128)S(1)}, s32[1,1,27,512]{3,1,2,0:T(1,128)}, u32[]{:S(2)}) copy-start(s32[1,1,27,512]{3,1,2,0:T(1,128)} %param.11) | copy-start | bytes 165892
  3.4 0.8 %copy-start.6 = (f32[1,1,3,5120]{3,1,2,0:T(1,128)S(1)}, f32[1,1,3,5120]{3,1,2,0:T(1,128)}, u32[]{:S(2)}) copy-start(f32[1,1,3,5120]{3,1,2,0:T(1,128)} %param.18) | copy-start | bytes 184324
  4.4 0.8 %copy-start.7 = (f32[1,1,3,5120]{3,1,2,0:T(1,128)S(1)}, f32[1,1,3,5120]{3,1,2,0:T(1,128)}, u32[]{:S(2)}) copy-start(f32[1,1,3,5120]{3,1,2,0:T(1,128)} %param.19) | copy-start | bytes 184324
  5.4 0.8 %copy-start = (s32[1,16,640]{2,1,0:T(8,128)S(1)}, s32[1,16,640]{2,1,0:T(8,128)}, u32[]{:S(2)}) copy-start(s32[1,16,640]{2,1,0:T(8,128)} %param.17) | copy-start | bytes 122884
  5.4 0.8 %copy-start.1 = (s32[1,1,2,384]{3,2,1,0:T(2,128)S(1)}, s32[1,1,2,384]{3,2,1,0:T(2,128)}, u32[]{:S(2)}) copy-start(s32[1,1,2,384]{3,2,1,0:T(2,128)} %param.16) | copy-start | bytes 9220
  5.4 0.8 %copy-start.2 = (s32[1,1,512]{2,1,0:T(1,128)S(1)}, s32[1,1,512]{2,1,0:T(1,128)}, u32[]{:S(2)}) copy-start(s32[1,1,512]{2,1,0:T(1,128)} %param.12) | copy-start | bytes 6148
  5.4 0.8 %copy-start.3 = (f32[1,1,512]{2,1,0:T(1,128)S(1)}, f32[1,1,512]{2,1,0:T(1,128)}, u32[]{:S(2)}) copy-start(f32[1,1,512]{2,1,0:T(1,128)} %param.13) | copy-start | bytes 6148
  5.4 0.8 %copy-start.4 = (bf16[32,288]{1,0:T(8,128)(2,1)S(1)}, bf16[32,288]{1,0:T(8,128)(2,1)}, u32[]{:S(2)}) copy-start(bf16[32,288]{1,0:T(8,128)(2,1)} %constant.5.clone.rev) | copy-start | bytes 55300
  5.4 0.8 %copy-start.5 = (bf16[96,96]{1,0:T(8,128)(2,1)S(1)}, bf16[96,96]{1,0:T(8,128)(2,1)}, u32[]{:S(2)}) copy-start(bf16[96,96]{1,0:T(8,128)(2,1)} %constant.4.clone.fwd) | copy-start | bytes 55300
